TPU v7x, 32 devices: a whole 2x2x4 slice. The times are simulated.
32 devices in a mesh: dom: 4 (over y, x), brick: 8 (over z, core).
Axes of the slice: x: 2, y: 2, z: 4, core: 2. Of those that a mesh axis runs over, the one named last changes fastest.
Arguments:
- positions: float32 [3, 2048, 128], P(None, ('dom', 'brick')), may hold values from 0 to 1
- direction: float32 [3, 2048, 128], P(None, ('dom', 'brick')), may hold values from -6 to 6
- pair_local: int32 [8192], P(('dom', 'brick')), may hold values from 0 to 63
- pair_peer: int32 [8192, 1], P(('dom', 'brick')), may hold values from 0 to 31; in each aligned block of 256 rows (0 to 255, 256 to 511, ...) at most 16 rows name the same one
- pair_remote: int32 [8192], P(('dom', 'brick')), may hold values from 0 to 63
- pair_mask: int32 [8192, 128], P(('dom', 'brick')), may hold values 0 or 1
Outputs:
- gradient: float32 [3, 2048, 128], P(None, ('dom', 'brick'))
- hess_dir: float32 [3, 2048, 128], P(None, ('dom', 'brick'))
Inputs may be any that keep to these rules, and one draw needn't show every extreme that they name: `pair_peer`: among the 256 rows of one device no device is named more than 16 times.
All inputs are finite; a program needn't handle non-finite values. No bound on the sum of `pair_mask` on one device may be relied on, other than what follows from the above.
Results may differ from a plain program's by a relative error of at most 0.0003.
Values sent between devices are 32-bit elements; how exact they have to be, the bound alone decides.
No kernel may reach another device: no remote copies, remote signals or barrier semaphores. Data moves between devices by JAX's collectives and lax.ppermute only.
A program may use at most 64 MiB of HBM per device.

v0:
```python
import functools

import jax
import jax.numpy as jnp
import numpy as np
from jax import lax
from jax.experimental import pallas as pl
from jax.experimental.pallas import tpu as pltpu
from jax.sharding import PartitionSpec as P

AXES = ("dom", "brick")
F32, BF16, I32 = jnp.float32, jnp.bfloat16, jnp.int32
GROUP = 8
LOG_SCALE = 2.0 * 0.6931471805599453
SMEM = pl.BlockSpec(memory_space=pltpu.SMEM)
VMEM = pl.BlockSpec(memory_space=pltpu.VMEM)
ANY = pl.BlockSpec(memory_space=pl.ANY)


def iota(shape, dim):
    return lax.broadcasted_iota(I32, shape, dim)


def params(mib):
    return pltpu.CompilerParams(vmem_limit_bytes=mib << 20)


def fetch(pairs, sems):
    copies = [pltpu.make_async_copy(src, dst, sems.at[i]) for i, (src, dst) in enumerate(pairs)]
    for copy in copies:
        copy.start()
    for copy in copies:
        copy.wait()


def weave_kernel(pos_hbm, dir_hbm, data_ref, pos_ref, dir_ref, sems):
    fetch([(pos_hbm, pos_ref), (dir_hbm, dir_ref)], sems)
    nblocks = pos_ref.shape[1]
    for c in range(3):
        data_ref[pl.ds(c, nblocks, stride=6), :] = pos_ref[c]
        data_ref[pl.ds(3 + c, nblocks, stride=6), :] = dir_ref[c]


def weave(positions, direction):
    nblocks = positions.shape[1]
    whole = pltpu.VMEM(positions.shape, F32)
    return pl.pallas_call(
        weave_kernel,
        out_shape=jax.ShapeDtypeStruct((nblocks * 6, 128), F32),
        in_specs=[ANY] * 2,
        out_specs=VMEM,
        scratch_shapes=[whole, whole, pltpu.SemaphoreType.DMA((2,))],
        compiler_params=params(16),
        name="weave",
    )(positions, direction)


def pack_kernel(
    ndev, slots, stride, peer_hbm, local_hbm, remote_hbm, mask_hbm, data_hbm, send_ref, mine_ref,
    peer_ref, local_ref, remote_ref, mask_ref, sems,
):
    fetch([(peer_hbm, peer_ref), (local_hbm, local_ref), (remote_hbm, remote_ref), (mask_hbm, mask_ref)], sems)
    npairs = peer_ref.shape[1]
    square = (npairs, npairs)
    rows, cols = iota(square, 0), iota(square, 1)

    def column(row):
        return jnp.sum(jnp.where(rows == cols, row, 0), axis=1, keepdims=True)

    peer = peer_ref[...]
    peer_col = column(peer)
    same = peer_col == peer
    rank = jnp.sum(jnp.where(same & (rows < cols), 1, 0), axis=0, keepdims=True)
    rank_col = jnp.sum(jnp.where(same & (cols < rows), 1, 0), axis=1, keepdims=True)
    local_col, remote_col = column(local_ref[...]), column(remote_ref[...])
    lane = iota((npairs, 128), 1)
    part, place = lane // slots, lane % slots
    pair = iota((npairs, 128), 0)
    value = jnp.where(part == 0, local_col, jnp.where(part == 1, remote_col, jnp.where(part == 2, pair, jnp.where(part == 3, 1, 0))))
    numbers = jnp.where(place == rank_col, value, 0).astype(F32).astype(BF16)
    mask = mask_ref[...].astype(F32).astype(BF16)
    slot = iota((ndev * stride, npairs), 0)
    hot = jnp.where(slot == peer * stride + rank, 1.0, 0.0).astype(BF16)
    hot_numbers = jnp.where(slot == peer * stride + slots, 1.0, 0.0).astype(BF16)
    send_ref[...] = jnp.dot(hot, mask, preferred_element_type=F32) + jnp.dot(hot_numbers, numbers, preferred_element_type=F32)
    hot_peer = jnp.where(iota((ndev, npairs), 0) == peer, 1.0, 0.0).astype(BF16)
    mine_ref[...] = jnp.dot(hot_peer, numbers, preferred_element_type=F32)


def pack(ndev, slots, stride, peer, local, remote, mask, data):
    row = pltpu.VMEM(peer.shape, I32)
    return pl.pallas_call(
        functools.partial(pack_kernel, ndev, slots, stride),
        out_shape=(jax.ShapeDtypeStruct((ndev * stride, 128), F32), jax.ShapeDtypeStruct((ndev, 128), F32)),
        in_specs=[ANY] * 5,
        out_specs=(VMEM,) * 2,
        scratch_shapes=[row, row, row, pltpu.VMEM(mask.shape, I32), pltpu.SemaphoreType.DMA((4,))],
        compiler_params=params(16),
        name="pack",
    )(peer, local, remote, mask, data)


def split(v):
    h = v.astype(BF16).astype(F32)
    e = v - h
    m = e.astype(BF16).astype(F32)
    return h, m, e - m


def products(d, h, m, row):
    both = h + m
    return both * jnp.where(row < 3, both, pltpu.roll(both, 3, 0))


def other_features(d, row):
    h, m, l = split(d)
    vh, vm, vl = split(products(d, h, m, row))
    hm = jnp.concatenate([h, m], 0).astype(BF16)
    vhm = jnp.concatenate([vh, vm], 0).astype(BF16)
    vlo = jnp.concatenate([vl, jnp.ones_like(d)], 0).astype(BF16)
    first = jnp.where(row < 6, h, jnp.where(row == 6, 1.0, pltpu.roll(l, 7, 0)))
    second = jnp.where(row < 6, m, pltpu.roll(l, 5, 0))
    return jnp.concatenate([hm, hm, vhm, vlo], 0), jnp.concatenate([first, second], 0)


def own_features(d, row):
    d = jnp.where(row < 6, d, 0.0)
    h, m, _ = split(d)
    v = products(d, h, m, row)
    total = v + pltpu.roll(v, 7, 0) + pltpu.roll(v, 6, 0)

    def parts(one_row):
        ph, pm, pl_ = split(jnp.broadcast_to(one_row, d.shape))
        return jnp.where(row == 0, ph, jnp.where(row == 1, pm, jnp.where(row == 2, pl_, 0.0)))

    def cross(a):
        return jnp.where(row < 3, -pltpu.roll(a, 5, 0), jnp.where(row < 6, -pltpu.roll(a, 3, 0), 0.0))

    hs, ms = jnp.where(row < 3, -2.0 * h, 0.0), jnp.where(row < 3, -2.0 * m, 0.0)
    hq, mq = cross(h), cross(m)
    low = jnp.where(row < 3, 1.0, 0.0)
    high = jnp.where((row >= 3) & (row < 6), 1.0, 0.0)
    for_s = jnp.concatenate([hs, ms, ms, hs, low, low, low, parts(total[0:1] + 0.1)], 0)
    for_q = jnp.concatenate([hq, mq, mq, hq, high, high, high, parts(total[3:4])], 0)
    return jnp.concatenate([for_s, for_q], 1).astype(BF16)


def plan_kernel(
    slots, stride, nlists, capacity, me_ref, table_ref, mine_ref, came_ref, mask_ref, data_ref,
    list_ref, count_ref, masks_ref, own_ref, code_vmem, code_smem, sem,
):
    ndev = mine_ref.shape[0]
    npairs = mask_ref.shape[0]
    nblocks = own_ref.shape[0]
    lane = iota((ndev, 128), 1)
    peer = iota((ndev, 128), 0)
    rel = iota((ndev, ndev), 0) ^ me_ref[0]
    entry = jnp.sum(jnp.where(iota((ndev, ndev), 1) == rel, table_ref[...], 0), axis=1, keepdims=True)
    which, unit = entry // 256, entry % 256

    def codes(numbers, mine):
        numbers = numbers.astype(I32)
        first = numbers
        second = pltpu.roll(numbers, 128 - slots, 1)
        third = pltpu.roll(numbers, 128 - 2 * slots, 1)
        used = jnp.where((lane >= 3 * slots) & (lane < 4 * slots), numbers, 0)
        count = jnp.sum(used, axis=1, keepdims=True)
        if mine:
            own, other, mask = first, second, third
        else:
            own, other, mask = second, first, npairs + peer * stride + lane
        code = (unit * nblocks + other) + own * (1 << 14) + mask * (1 << 20)
        return jnp.where(lane < slots, code, jnp.where(lane == slots, count, which))

    code_vmem[0:ndev, :] = codes(mine_ref[...], True)
    code_vmem[ndev:, :] = codes(came_ref[pl.ds(slots, ndev, stride=stride), :], False)
    copy = pltpu.make_async_copy(code_vmem, code_smem, sem)
    copy.start()
    masks_ref[0:npairs, :] = mask_ref[...].astype(F32)
    masks_ref[npairs : npairs + ndev * stride, :] = came_ref[...]
    masks_ref[npairs + ndev * stride :, :] = jnp.zeros((8, 128), F32)
    row = iota((8, 128), 0)

    def feature(i, _):
        for u in range(4):
            b = i * 4 + u
            start = jnp.minimum(b * 6, nblocks * 6 - 8)
            d = data_ref[pl.ds(start, 8), :]
            d = jnp.where(b == nblocks - 1, pltpu.roll(d, 6, 0), d)
            own_ref[b] = own_features(d, row)
        return 0

    lax.fori_loop(0, nblocks // 4, feature, 0)
    copy.wait()
    for k in range(nlists):
        count_ref[k] = 0

    def fill(p, _):
        k = code_smem[p, slots + 1]
        at = count_ref[k]
        for r in range(slots):
            list_ref[k * capacity + at + r] = code_smem[p, r]
        count_ref[k] = at + code_smem[p, slots]
        return 0

    lax.fori_loop(0, 2 * ndev, fill, 0)
    for k in range(nlists):
        at = count_ref[k]
        for r in range(GROUP):
            list_ref[k * capacity + at + r] = (npairs + ndev * stride) * (1 << 20)


def plan(slots, stride, nlists, me, table, mine, came, mask, data):
    ndev, npairs, nblocks = mine.shape[0], mask.shape[0], data.shape[0] // 6
    capacity = npairs + ndev * slots + slots + GROUP
    out = pl.pallas_call(
        functools.partial(plan_kernel, slots, stride, nlists, capacity),
        out_shape=(
            jax.ShapeDtypeStruct((nlists * capacity,), I32),
            jax.ShapeDtypeStruct((nlists,), I32),
            jax.ShapeDtypeStruct((npairs + ndev * stride + 8, 128), F32),
            jax.ShapeDtypeStruct((nblocks, 64, 256), BF16),
        ),
        in_specs=[SMEM] + [VMEM] * 5,
        out_specs=(SMEM, SMEM, VMEM, VMEM),
        scratch_shapes=[pltpu.VMEM((2 * ndev, 128), I32), pltpu.SMEM((2 * ndev, 128), I32), pltpu.SemaphoreType.DMA],
        compiler_params=params(16),
        name="plan",
    )(me, table, mine, came, mask, data)
    return capacity, out


def halves(c):
    h = c.astype(BF16)
    return h, (c - h.astype(F32)).astype(BF16)


def prepare(codes, block_ref, masks_ref, npairs, k_ref, f_ref):
    row = iota((8, 128), 0)
    for g, code in enumerate(codes):
        d = block_ref[pl.ds((code & 0x3FFF) * 6, 8), :]
        left, sums = other_features(d, row)
        place = code >> 20
        mask = jnp.where(place < npairs, 1.0, masks_ref[pl.ds(place, 1), :])
        f_ref[g] = (sums * mask).astype(BF16)
        k_ref[g] = left.T


def accumulate(codes, own_ref, masks_ref, npairs, acc_ref, k_ref, f_ref):
    outs = []
    for g, code in enumerate(codes):
        own = (code >> 14) & 63
        both = jnp.dot(k_ref[g], own_ref[own], preferred_element_type=F32)
        s = jnp.minimum(both[:, :128], 1.0)
        gap = s - 1.0
        log = LOG_SCALE * jnp.log2(s)
        ratio = gap * pl.reciprocal(s, approx=True)
        one = gap * (log + ratio)
        two = ((ratio - 4.0) * ratio - log) * both[:, 128:]
        one_h, one_l = halves(one)
        two_h, two_l = halves(two)
        weights = jnp.concatenate([jnp.concatenate([one_h, two_h], 1), jnp.concatenate([one_l, two_l], 1)], 0)
        f = f_ref[g]
        out = jnp.dot(jnp.concatenate([f, f], 1), weights, preferred_element_type=F32)
        place = code >> 20
        mask = jnp.where(place < npairs, masks_ref[pl.ds(place, 1), :], 1.0)
        outs.append((own, out * jnp.concatenate([mask, mask], 1)))
    for own, out in outs:
        acc_ref[own] += out


def finish(data_ref, acc_ref, grad_ref, hess_ref):
    nblocks = acc_ref.shape[0]
    row = iota((8, 128), 0)

    def block(b, _):
        start = jnp.minimum(b * 6, nblocks * 6 - 8)
        d = data_ref[pl.ds(start, 8), :]
        d = jnp.where(b == nblocks - 1, pltpu.roll(d, 6, 0), d)
        acc = acc_ref[b]

        def sums(a):
            first, second = a[0:8], a[8:16]
            total = first + second
            low = jnp.where(row == 0, pltpu.roll(first, 1, 0), jnp.where(row < 3, pltpu.roll(second, 3, 0), 0.0))
            return first[6:7], total + low

        n_one, y_one = sums(acc[:, :128] * -0.01)
        n_two, y_two = sums(acc[:, 128:] * 0.02)
        a = d * n_one - y_one
        c = d * n_two - y_two + pltpu.roll(a, 5, 0)
        for k in range(3):
            grad_ref[k, pl.ds(b, 1), :] = a[k : k + 1]
            hess_ref[k, pl.ds(b, 1), :] = c[k : k + 1]
        return 0

    lax.fori_loop(0, nblocks, block, 0)


def task_kernel(lists, capacity, npairs, first, last, *refs):
    list_ref, count_ref, masks_ref, own_ref, data_ref = refs[:5]
    blocks, refs = refs[5 : 5 + len(lists)], refs[5 + len(lists) :]
    if not first:
        before_ref, refs = refs[0], refs[1:]
    if last:
        grad_ref, hess_ref, acc_ref, k_ref, f_ref = refs
    else:
        acc_ref, k_ref, f_ref = refs
    if first:
        acc_ref[...] = jnp.zeros_like(acc_ref)
    else:
        acc_ref[...] = before_ref[...]
    for k, block_ref in zip(lists, blocks):
        count = count_ref[k]
        groups = (count + GROUP - 1) // GROUP

        def codes(i, k=k):
            return [list_ref[k * capacity + i * GROUP + g] for g in range(GROUP)]

        @pl.when(groups > 0)
        def _(block_ref=block_ref, codes=codes, groups=groups):
            prepare(codes(0), block_ref, masks_ref, npairs, k_ref, f_ref)

            def step(i, _):
                accumulate(codes(i), own_ref, masks_ref, npairs, acc_ref, k_ref, f_ref)
                prepare(codes(jnp.minimum(i + 1, groups - 1)), block_ref, masks_ref, npairs, k_ref, f_ref)
                return 0

            lax.fori_loop(0, groups, step, 0)

    if last:
        finish(data_ref, acc_ref, grad_ref, hess_ref)


def tasks(lists, capacity, npairs, list_, count, masks, own, data, blocks, before, last):
    nblocks = own.shape[0]
    acc = jax.ShapeDtypeStruct((nblocks, 16, 256), F32)
    out = jax.ShapeDtypeStruct((3, nblocks, 128), F32)
    first = before is None
    scratch = [pltpu.VMEM((GROUP, 128, 64), BF16), pltpu.VMEM((GROUP, 16, 128), BF16)]
    if last:
        scratch = [pltpu.VMEM(acc.shape, F32)] + scratch
    args = [list_, count, masks, own, data, *blocks] + ([] if first else [before])
    size = sum(b.size for b in blocks) * 4
    return pl.pallas_call(
        functools.partial(task_kernel, lists, capacity, npairs, first, last),
        out_shape=(out, out) if last else acc,
        in_specs=[SMEM, SMEM] + [VMEM] * (len(args) - 2),
        out_specs=(VMEM, VMEM) if last else VMEM,
        scratch_shapes=scratch,
        compiler_params=params(24),
        cost_estimate=pl.CostEstimate(flops=size * 2000, bytes_accessed=size * 3, transcendentals=0),
        name="tasks",
    )(*args)


class Piece:
    def __init__(self, tags, array):
        self.tags, self.array = list(tags), array

    def cut(self, start, stop):
        rows = self.array.shape[0] // len(self.tags)
        return Piece(self.tags[start:stop], self.array[start * rows : stop * rows])


def join(pieces):
    if len(pieces) == 1:
        return pieces[0]
    return Piece(sum([p.tags for p in pieces], []), jnp.concatenate([p.array for p in pieces], axis=0))


def swap(piece, bit, ndev):
    pairs = [(i, i ^ (1 << bit)) for i in range(ndev)]
    return Piece([t ^ (1 << bit) for t in piece.tags], lax.ppermute(piece.array, AXES, pairs))


def tie(piece, other):
    array, _ = lax.optimization_barrier((piece.array, other))
    return Piece(piece.tags, array)


def on_device(positions, direction, pair_local, pair_peer, pair_remote, pair_mask):
    npairs = pair_local.shape[0]
    nblocks = positions.shape[1]
    ndev = lax.axis_size(AXES)
    me = lax.axis_index(AXES).astype(I32)
    slots = max(2, 2 * npairs // ndev)
    stride = -(-(slots + 1) // 8) * 8
    peer, local, remote = (a.reshape(1, npairs) for a in (pair_peer, pair_local, pair_remote))
    data = weave(positions, direction)
    send, mine = pack(ndev, slots, stride, peer, local, remote, pair_mask, data)
    came = lax.all_to_all(send, AXES, split_axis=0, concat_axis=0, tiled=True)

    bits = ndev.bit_length() - 1
    x, y = bits - 2, bits - 1
    column = Piece([0], data)
    for bit in range(bits - 3, 0, -1):
        column = join([column, swap(column, bit, ndev)])
    column.array, came = lax.optimization_barrier((column.array, came))
    over_x, over_y = swap(column, x, ndev), swap(column, y, ndev)
    half = len(column.tags) // 2

    table = np.zeros((1, ndev), np.int32)
    tail = Piece([], jnp.zeros((8, 128), F32))

    def both(k, pieces):
        near = join(pieces + [tail])
        far = swap(near, 0, ndev)
        for which, p in ((2 * k, near), (2 * k + 1, far)):
            for unit, tag in enumerate(p.tags):
                table[0, tag] = which * 256 + unit
        return near.array, far.array

    shape = [
        [column],
        [Piece([t ^ (1 << x) for t in column.tags], None), Piece([t ^ (1 << y) for t in column.tags], None)],
    ]
    diagonal = [t ^ (1 << x) ^ (1 << y) for t in column.tags]
    shape.append([Piece(diagonal[:half], None), Piece(diagonal[half:], None)])
    for k, pieces in enumerate(shape):
        tags = sum([p.tags for p in pieces], [])
        for unit, tag in enumerate(tags):
            table[0, tag] = 2 * k * 256 + unit
            table[0, tag ^ 1] = (2 * k + 1) * 256 + unit
    nlists = 6
    capacity, (list_, count, masks, own) = plan(
        slots, stride, nlists, me.reshape(1), jnp.asarray(table), mine, came, pair_mask, data
    )
    run = functools.partial(tasks, capacity=capacity, npairs=npairs, list_=list_, count=count, masks=masks, own=own, data=data)

    near, far = both(0, [column])
    acc = run(lists=(0, 1), blocks=(near, far), before=None, last=False)
    over_x, over_y = tie(over_x, acc), tie(over_y, acc)
    corner_x, corner_y = swap(over_y.cut(0, half), x, ndev), swap(over_x.cut(half, 2 * half), y, ndev)
    near, far = both(1, [over_x, over_y])
    acc = run(lists=(2,), blocks=(near,), before=acc, last=False)
    acc = run(lists=(3,), blocks=(far,), before=acc, last=False)
    corner_x, corner_y = tie(corner_x, acc), tie(corner_y, acc)
    near, far = both(2, [corner_x, corner_y])
    acc = run(lists=(4,), blocks=(near,), before=acc, last=False)
    return run(lists=(5,), blocks=(far,), before=acc, last=True)


def solution(mesh):
    blocked = P(None, AXES, None)
    in_specs = (blocked, blocked, P(AXES), P(AXES, None), P(AXES), P(AXES, None))
    return jax.shard_map(on_device, mesh=mesh, in_specs=in_specs, out_specs=(blocked, blocked), check_vma=False)
```

profile of v0, /device:TPU:27, one launch (start us, length us, event | category | flops | bytes accessed | tf_op | source)
XLA Modules:
  0.0 107.9 jit_solution(6208087707391457174)
XLA Ops:
  0.6 0.9 copy-done.2
  1.5 0.9 copy-done.3
  2.4 0.3 weave.1.data_hbm.data_ref.refs_4_
  2.7 0.1 collective-permute-start
  2.8 0.9 copy-done
  3.7 0.7 copy-done.4
  4.4 0.7 copy-done.5
  5.1 0.7 copy-done.6
  5.7 1.7 %pack.1 = (f32[768,128]{1,0:T(8,128)}, f32[32,128]{1,0:T(8,128)S(1)}) custom-call(s32[1,256]{1,0:T(1,128)S(1)} %bitcast.7, s32[1,256]{1,0:T(1,128)S(1)} %bitcast.8, s32[1,256]{1,0:T(1,128)S(1)} %bitcast.9, s32[256,128]{1,0:T(8,128)S(1)} %copy-done, f32[384,128]{1,0:T(8,128)S(1)} %weave.1.data_hbm.data_ref.refs_4_), custom_call_target="tpu_custom_call" | custom-call | tf_op jit(solution)/shard_map/pack/pallas_call | solution.py:92
  7.4 6.7 %all-to-all-start = ((f32[32,24,128]{2,1,0:T(8,128)}), f32[32,24,128]{2,1,0:T(8,128)S(1)}, u32[]{:S(2)}, u32[]{:S(2)}) async-start(f32[32,24,128]{2,1,0:T(8,128)} %bitcast.4), calls=%async_computation | async-start | bytes 786432 | tf_op jit(solution)/shard_map/all_to_all | solution.py:392
  14.1 0.5 collective-permute-done
  14.6 0.1 collective-permute-start.1
  14.7 15.5 %collective-permute-done.1 = f32[768,128]{1,0:T(8,128)S(1)} collective-permute-done((f32[768,128]{1,0:T(8,128)S(1)}, f32[768,128]{1,0:T(8,128)S(1)}, u32[]{:S(2)}, u32[]{:S(2)}) %collective-permute-start.1) | collective-permute-done | bytes 393248 | tf_op jit(solution)/shard_map/ppermute | solution.py:374
  30.1 0.1 pad_maximum_fusion.2
  30.2 0.1 concatenate.18.refs_5_
  30.3 0.7 collective-permute-start.3
  31.0 0.2 collective-permute-start.5
  31.2 1.3 %collective-permute-start.2 = (f32[1536,128]{1,0:T(8,128)S(1)}, f32[1536,128]{1,0:T(8,128)}, u32[]{:S(2)}, u32[]{:S(2)}) collective-permute-start(f32[1536,128]{1,0:T(8,128)S(1)} %pad_maximum_fusion.2), channel_id=1, source_target_pairs={{0,16},{1,17},{2,18},{3,19},{4,20},{5,21},{6,22},{7,23},{8,24},{9,... | collective-permute-start | bytes 2359304 | tf_op jit(solution)/shard_map/ppermute | solution.py:374
  32.5 3.7 %plan.1 = (s32[4752]{0:T(1024)S(1)}, s32[6]{0:T(128)S(1)}, f32[1032,128]{1,0:T(8,128)S(1)}, bf16[64,64,256]{2,1,0:T(8,128)(2,1)S(1)}) custom-call(s32[1]{0:T(128)} %bitcast.me_ref, s32[1,32]{1,0:T(1,128)S(1)} %copy-done.7, f32[32,128]{1,0:T(8,128)S(1)} %get-tuple-element.14.mine_ref, f32[768,128]{1,0:T(8,128)S(1)} %bitcast.6, s32[256,128]{1,0:T(8,128)S(1)} %copy-done.1, ...), custom_call_target="tpu_custom_call" | custom-call | tf_op jit(solution)/shard_map/plan/pallas_call | solution.py:216
  36.2 15.6 %tasks.5.refs_6_ = f32[64,16,256]{2,1,0:T(8,128)S(1)} custom-call(s32[4752]{0:T(1024)S(1)} %get-tuple-element.17.refs_0_, s32[6]{0:T(128)S(1)} %get-tuple-element.18.refs_1_, f32[1032,128]{1,0:T(8,128)S(1)} %get-tuple-element.19.refs_2_, bf16[64,64,256]{2,1,0:T(8,128)(2,1)S(1)} %get-tuple-element.20.refs_3_, f32[384,128]{1,0:T(8,128)S(1)} %weave.1.data_hbm.data_ref.refs_4_, ...), custom_call_target="tpu_custom_call" | custom-call | flops 3162112000 | bytes 4743168 | tf_op jit(solution)/shard_map/tasks/pallas_call | solution.py:345
  51.9 1.5 %pad_maximum_fusion.refs_5_ = f32[3080,128]{1,0:T(8,128)S(1)} fusion(f32[8,128]{1,0:T(8,128)S(1)} %broadcast_in_dim.3, f32[1536,128]{1,0:T(8,128)} %collective-permute-done.2, f32[1536,128]{1,0:T(8,128)} %collective-permute-done.5), kind=kLoop, calls=%fused_computation | loop fusion | flops 788480 | bytes 3153920 | tf_op jit(solution)/shard_map/concatenate | solution.py:369
  53.3 1.9 %collective-permute-start.6 = (f32[3080,128]{1,0:T(8,128)S(1)}, f32[3080,128]{1,0:T(8,128)S(1)}, u32[]{:S(2)}, u32[]{:S(2)}) collective-permute-start(f32[3080,128]{1,0:T(8,128)S(1)} %pad_maximum_fusion.refs_5_), channel_id=1, source_target_pairs={{0,1},{1,0},{2,3},{3,2},{4,5},{5,4},{6,7},{7,6},{8,9},{9,8},{10,11... | collective-permute-start | bytes 4730888 | tf_op jit(solution)/shard_map/ppermute | solution.py:374
  55.2 1.0 slice.6
  56.3 1.0 slice.7
  57.3 0.1 collective-permute-start.7
  57.4 0.2 collective-permute-start.4
  57.6 14.9 %tasks.6.refs_6_ = f32[64,16,256]{2,1,0:T(8,128)S(1)} custom-call(s32[4752]{0:T(1024)S(1)} %get-tuple-element.17.refs_0_, s32[6]{0:T(128)S(1)} %get-tuple-element.18.refs_1_, f32[1032,128]{1,0:T(8,128)S(1)} %get-tuple-element.19.refs_2_, bf16[64,64,256]{2,1,0:T(8,128)(2,1)S(1)} %get-tuple-element.20.refs_3_, f32[384,128]{1,0:T(8,128)S(1)} %weave.1.data_hbm.data_ref.refs_4_, ...), custom_call_target="tpu_custom_call" | custom-call | flops 3153920000 | bytes 4730880 | tf_op jit(solution)/shard_map/tasks/pallas_call | solution.py:345
  72.5 14.3 %tasks.7.refs_6_ = f32[64,16,256]{2,1,0:T(8,128)S(1)} custom-call(s32[4752]{0:T(1024)S(1)} %get-tuple-element.17.refs_0_, s32[6]{0:T(128)S(1)} %get-tuple-element.18.refs_1_, f32[1032,128]{1,0:T(8,128)S(1)} %get-tuple-element.19.refs_2_, bf16[64,64,256]{2,1,0:T(8,128)(2,1)S(1)} %get-tuple-element.20.refs_3_, f32[384,128]{1,0:T(8,128)S(1)} %weave.1.data_hbm.data_ref.refs_4_, ...), custom_call_target="tpu_custom_call" | custom-call | flops 3153920000 | bytes 4730880 | tf_op jit(solution)/shard_map/tasks/pallas_call | solution.py:345
  86.9 0.1 pad_maximum_fusion.1.refs_5_
  87.0 2.3 %collective-permute-start.8 = (f32[1544,128]{1,0:T(8,128)S(1)}, f32[1544,128]{1,0:T(8,128)S(1)}, u32[]{:S(2)}, u32[]{:S(2)}) collective-permute-start(f32[1544,128]{1,0:T(8,128)S(1)} %pad_maximum_fusion.1.refs_5_), channel_id=1, source_target_pairs={{0,1},{1,0},{2,3},{3,2},{4,5},{5,4},{6,7},{7,6},{8,9},{9,8},{10,11... | collective-permute-start | bytes 2371592 | tf_op jit(solution)/shard_map/ppermute | solution.py:374
  89.3 7.7 %tasks.8.refs_6_ = f32[64,16,256]{2,1,0:T(8,128)S(1)} custom-call(s32[4752]{0:T(1024)S(1)} %get-tuple-element.17.refs_0_, s32[6]{0:T(128)S(1)} %get-tuple-element.18.refs_1_, f32[1032,128]{1,0:T(8,128)S(1)} %get-tuple-element.19.refs_2_, bf16[64,64,256]{2,1,0:T(8,128)(2,1)S(1)} %get-tuple-element.20.refs_3_, f32[384,128]{1,0:T(8,128)S(1)} %weave.1.data_hbm.data_ref.refs_4_, ...), custom_call_target="tpu_custom_call" | custom-call | flops 1581056000 | bytes 2371584 | tf_op jit(solution)/shard_map/tasks/pallas_call | solution.py:345
  97.0 10.9 %tasks.9 = (f32[3,64,128]{2,1,0:T(8,128)}, f32[3,64,128]{2,1,0:T(8,128)}) custom-call(s32[4752]{0:T(1024)S(1)} %get-tuple-element.17.refs_0_, s32[6]{0:T(128)S(1)} %get-tuple-element.18.refs_1_, f32[1032,128]{1,0:T(8,128)S(1)} %get-tuple-element.19.refs_2_, bf16[64,64,256]{2,1,0:T(8,128)(2,1)S(1)} %get-tuple-element.20.refs_3_, ...), custom_call_target="tpu_custom_call" | custom-call | flops 1581056000 | bytes 2371584 | tf_op jit(solution)/shard_map/tasks/pallas_call | solution.py:345
  (20 shorter events, 0.1 us)
Async XLA Ops:
  0.6 0.9 copy-start.2
  1.5 0.9 copy-start.3
  2.7 11.9 %collective-permute-start = (f32[384,128]{1,0:T(8,128)S(1)}, f32[384,128]{1,0:T(8,128)S(1)}, u32[]{:S(2)}, u32[]{:S(2)}) collective-permute-start(f32[384,128]{1,0:T(8,128)S(1)} %weave.1.data_hbm.data_ref.refs_4_), channel_id=1, source_target_pairs={{0,4},{1,5},{2,6},{3,7},{4,0},{5,1},{6,2},{7,3},{8,12},{9,13},{10,... | collective-permute-start | bytes 589832 | tf_op jit(solution)/shard_map/ppermute | solution.py:374
  2.8 0.9 copy-start
  3.7 0.7 copy-start.4
  4.4 0.7 copy-start.5
  5.1 0.7 copy-start.6
  7.4 22.8 %all-to-all-start = ((f32[32,24,128]{2,1,0:T(8,128)}), f32[32,24,128]{2,1,0:T(8,128)S(1)}, u32[]{:S(2)}, u32[]{:S(2)}) async-start(f32[32,24,128]{2,1,0:T(8,128)} %bitcast.4), calls=%async_computation | async-start | bytes 786432 | tf_op jit(solution)/shard_map/all_to_all | solution.py:392
  14.6 17.9 %copy-start.1 = (s32[256,128]{1,0:T(8,128)S(1)}, s32[256,128]{1,0:T(8,128)}, u32[]{:S(2)}) copy-start(s32[256,128]{1,0:T(8,128)} %mask_ref.1) | copy-start | bytes 393220
  14.6 17.9 %copy-start.7 = (s32[1,32]{1,0:T(1,128)S(1)}, s32[1,32]{1,0:T(1,128)}, u32[]{:S(2)}) copy-start(s32[1,32]{1,0:T(1,128)} %constant.14.clone.table_ref) | copy-start | bytes 388
  14.6 15.5 %collective-permute-start.1 = (f32[768,128]{1,0:T(8,128)S(1)}, f32[768,128]{1,0:T(8,128)S(1)}, u32[]{:S(2)}, u32[]{:S(2)}) collective-permute-start(f32[768,128]{1,0:T(8,128)S(1)} %pad_maximum_fusion.3), channel_id=1, source_target_pairs={{0,2},{1,3},{2,0},{3,1},{4,6},{5,7},{6,4},{7,5},{8,10},{9,11},{10,... | collective-permute-start | bytes 1179656 | tf_op jit(solution)/shard_map/ppermute | solution.py:374
  30.3 5.9 %collective-permute-start.3 = (f32[1544,128]{1,0:T(8,128)S(1)}, f32[1544,128]{1,0:T(8,128)S(1)}, u32[]{:S(2)}, u32[]{:S(2)}) collective-permute-start(f32[1544,128]{1,0:T(8,128)S(1)} %concatenate.18.refs_5_), channel_id=1, source_target_pairs={{0,1},{1,0},{2,3},{3,2},{4,5},{5,4},{6,7},{7,6},{8,9},{9,8},{10,11... | collective-permute-start | bytes 2371592 | tf_op jit(solution)/shard_map/ppermute | solution.py:374
  31.0 20.8 %collective-permute-start.5 = (f32[1536,128]{1,0:T(8,128)S(1)}, f32[1536,128]{1,0:T(8,128)}, u32[]{:S(2)}, u32[]{:S(2)}) collective-permute-start(f32[1536,128]{1,0:T(8,128)S(1)} %pad_maximum_fusion.2), channel_id=1, source_target_pairs={{0,8},{1,9},{2,10},{3,11},{4,12},{5,13},{6,14},{7,15},{8,0},{9,1},... | collective-permute-start | bytes 2359304 | tf_op jit(solution)/shard_map/ppermute | solution.py:374
  31.2 20.7 %collective-permute-start.2 = (f32[1536,128]{1,0:T(8,128)S(1)}, f32[1536,128]{1,0:T(8,128)}, u32[]{:S(2)}, u32[]{:S(2)}) collective-permute-start(f32[1536,128]{1,0:T(8,128)S(1)} %pad_maximum_fusion.2), channel_id=1, source_target_pairs={{0,16},{1,17},{2,18},{3,19},{4,20},{5,21},{6,22},{7,23},{8,24},{9,... | collective-permute-start | bytes 2359304 | tf_op jit(solution)/shard_map/ppermute | solution.py:374
  53.3 19.2 %collective-permute-start.6 = (f32[3080,128]{1,0:T(8,128)S(1)}, f32[3080,128]{1,0:T(8,128)S(1)}, u32[]{:S(2)}, u32[]{:S(2)}) collective-permute-start(f32[3080,128]{1,0:T(8,128)S(1)} %pad_maximum_fusion.refs_5_), channel_id=1, source_target_pairs={{0,1},{1,0},{2,3},{3,2},{4,5},{5,4},{6,7},{7,6},{8,9},{9,8},{10,11... | collective-permute-start | bytes 4730888 | tf_op jit(solution)/shard_map/ppermute | solution.py:374
  57.3 29.6 %collective-permute-start.7 = (f32[768,128]{1,0:T(8,128)S(1)}, f32[768,128]{1,0:T(8,128)S(1)}, u32[]{:S(2)}, u32[]{:S(2)}) collective-permute-start(f32[768,128]{1,0:T(8,128)S(1)} %slice.7), channel_id=1, source_target_pairs={{0,16},{1,17},{2,18},{3,19},{4,20},{5,21},{6,22},{7,23},{8,24},{9,... | collective-permute-start | bytes 1179656 | tf_op jit(solution)/shard_map/ppermute | solution.py:374
  57.4 29.5 %collective-permute-start.4 = (f32[768,128]{1,0:T(8,128)S(1)}, f32[768,128]{1,0:T(8,128)S(1)}, u32[]{:S(2)}, u32[]{:S(2)}) collective-permute-start(f32[768,128]{1,0:T(8,128)S(1)} %slice.6), channel_id=1, source_target_pairs={{0,8},{1,9},{2,10},{3,11},{4,12},{5,13},{6,14},{7,15},{8,0},{9,1},... | collective-permute-start | bytes 1179656 | tf_op jit(solution)/shard_map/ppermute | solution.py:374
  87.0 10.0 %collective-permute-start.8 = (f32[1544,128]{1,0:T(8,128)S(1)}, f32[1544,128]{1,0:T(8,128)S(1)}, u32[]{:S(2)}, u32[]{:S(2)}) collective-permute-start(f32[1544,128]{1,0:T(8,128)S(1)} %pad_maximum_fusion.1.refs_5_), channel_id=1, source_target_pairs={{0,1},{1,0},{2,3},{3,2},{4,5},{5,4},{6,7},{7,6},{8,9},{9,8},{10,11... | collective-permute-start | bytes 2371592 | tf_op jit(solution)/shard_map/ppermute | solution.py:374
where the time goes:
time: 109 us; the launch traced here: 108 us
  Pallas kernels  69 us (63%)
  waiting for transfers between devices  15.9 us (15%)
  starting transfers between devices  13.6 us (12%)
  local copies, waits for them, and re-layouts  6.83 us (6%)
  other arithmetic  1.61 us (1%)
    pallas_call x5, Pallas kernels, tasks(): pl.pallas_call(functools.partial(task_kernel, lists, capacity, npairs, fi...  63.5 us
    ppermute x9, waiting for transfers between devices, swap(): lax.ppermute(piece.array, AXES, pairs)  15.9 us
    ppermute x9, starting transfers between devices, swap(): lax.ppermute(piece.array, AXES, pairs)  6.91 us
    all_to_all x1, starting transfers between devices, on_device(): came = lax.all_to_all(send, AXES, split_axis=0, concat_axis=0, tiled=True)  6.68 us
    unnamed x16, local copies, waits for them, and re-layouts  4.73 us
    pallas_call x1, Pallas kernels, plan(): pl.pallas_call(functools.partial(plan_kernel, slots, stride, nlists, capa...  3.69 us
  transfers between devices with their start and end apart: 10, of which 2 were waited for; matrix products, arithmetic and copies ran while one was open for 2% of the time, Pallas kernels for 54%

commit v1 on v0

--- a/solution.py
+++ b/solution.py
@@ -10,10 +10,11 @@
 
 AXES = ("dom", "brick")
 F32, BF16, I32 = jnp.float32, jnp.bfloat16, jnp.int32
-GROUP = 8
+GROUP = 16
 LOG_SCALE = 2.0 * 0.6931471805599453
 SMEM = pl.BlockSpec(memory_space=pltpu.SMEM)
 VMEM = pl.BlockSpec(memory_space=pltpu.VMEM)
+HBM = pl.BlockSpec(memory_space=pltpu.HBM)
 ANY = pl.BlockSpec(memory_space=pl.ANY)
 
 
@@ -47,10 +48,10 @@
     return pl.pallas_call(
         weave_kernel,
         out_shape=jax.ShapeDtypeStruct((nblocks * 6, 128), F32),
-        in_specs=[ANY] * 2,
+        in_specs=[HBM] * 2,
         out_specs=VMEM,
         scratch_shapes=[whole, whole, pltpu.SemaphoreType.DMA((2,))],
-        compiler_params=params(16),
+        compiler_params=params(60),
         name="weave",
     )(positions, direction)
 
@@ -92,12 +93,19 @@
     return pl.pallas_call(
         functools.partial(pack_kernel, ndev, slots, stride),
         out_shape=(jax.ShapeDtypeStruct((ndev * stride, 128), F32), jax.ShapeDtypeStruct((ndev, 128), F32)),
-        in_specs=[ANY] * 5,
+        in_specs=[HBM] * 4 + [ANY],
         out_specs=(VMEM,) * 2,
         scratch_shapes=[row, row, row, pltpu.VMEM(mask.shape, I32), pltpu.SemaphoreType.DMA((4,))],
-        compiler_params=params(16),
+        compiler_params=params(60),
         name="pack",
     )(peer, local, remote, mask, data)
+
+
+def load_block(ref, block):
+    last = ref.shape[0] - 8
+    start = block * 6
+    d = ref[pl.ds(jnp.minimum(start, last), 8), :]
+    return jnp.where(start > last, pltpu.roll(d, 6, 0), d)
 
 
 def split(v):
@@ -145,32 +153,53 @@
     return jnp.concatenate([for_s, for_q], 1).astype(BF16)
 
 
+def feature_kernel(data_ref, own_ref):
+    row = iota((8, 128), 0)
+
+    def feature(i, _):
+        for u in range(4):
+            own_ref[i * 4 + u] = own_features(load_block(data_ref, i * 4 + u), row)
+        return 0
+
+    lax.fori_loop(0, own_ref.shape[0] // 4, feature, 0)
+
+
+def features(data):
+    nblocks = data.shape[0] // 6
+    return pl.pallas_call(
+        feature_kernel,
+        out_shape=jax.ShapeDtypeStruct((nblocks, 64, 256), BF16),
+        in_specs=[VMEM],
+        out_specs=VMEM,
+        compiler_params=params(16),
+        name="features",
+    )(data)
+
+
 def plan_kernel(
-    slots, stride, nlists, capacity, me_ref, table_ref, mine_ref, came_ref, mask_ref, data_ref,
-    list_ref, count_ref, masks_ref, own_ref, code_vmem, code_smem, sem,
+    slots, stride, sizes, me_ref, order_ref, table_ref, mine_ref, came_ref, mask_ref,
+    list_ref, where_ref, masks_ref, code_vmem, code_smem, sem,
 ):
     ndev = mine_ref.shape[0]
     npairs = mask_ref.shape[0]
-    nblocks = own_ref.shape[0]
+    me = me_ref[0]
     lane = iota((ndev, 128), 1)
     peer = iota((ndev, 128), 0)
-    rel = iota((ndev, ndev), 0) ^ me_ref[0]
-    entry = jnp.sum(jnp.where(iota((ndev, ndev), 1) == rel, table_ref[...], 0), axis=1, keepdims=True)
-    which, unit = entry // 256, entry % 256
+    rel = iota((ndev, ndev), 0) ^ me
+    first_block = jnp.sum(jnp.where(iota((ndev, ndev), 1) == rel, table_ref[...], 0), axis=1, keepdims=True)
 
     def codes(numbers, mine):
         numbers = numbers.astype(I32)
-        first = numbers
         second = pltpu.roll(numbers, 128 - slots, 1)
         third = pltpu.roll(numbers, 128 - 2 * slots, 1)
         used = jnp.where((lane >= 3 * slots) & (lane < 4 * slots), numbers, 0)
         count = jnp.sum(used, axis=1, keepdims=True)
         if mine:
-            own, other, mask = first, second, third
+            own, other, mask = numbers, second, third
         else:
-            own, other, mask = second, first, npairs + peer * stride + lane
-        code = (unit * nblocks + other) + own * (1 << 14) + mask * (1 << 20)
-        return jnp.where(lane < slots, code, jnp.where(lane == slots, count, which))
+            own, other, mask = second, numbers, npairs + peer * stride + lane
+        code = (first_block + other) + own * (1 << 14) + mask * (1 << 20)
+        return jnp.where(lane < slots, code, count)
 
     code_vmem[0:ndev, :] = codes(mine_ref[...], True)
     code_vmem[ndev:, :] = codes(came_ref[pl.ds(slots, ndev, stride=stride), :], False)
@@ -179,55 +208,48 @@
     masks_ref[0:npairs, :] = mask_ref[...].astype(F32)
     masks_ref[npairs : npairs + ndev * stride, :] = came_ref[...]
     masks_ref[npairs + ndev * stride :, :] = jnp.zeros((8, 128), F32)
-    row = iota((8, 128), 0)
-
-    def feature(i, _):
-        for u in range(4):
-            b = i * 4 + u
-            start = jnp.minimum(b * 6, nblocks * 6 - 8)
-            d = data_ref[pl.ds(start, 8), :]
-            d = jnp.where(b == nblocks - 1, pltpu.roll(d, 6, 0), d)
-            own_ref[b] = own_features(d, row)
-        return 0
-
-    lax.fori_loop(0, nblocks // 4, feature, 0)
     copy.wait()
-    for k in range(nlists):
-        count_ref[k] = 0
-
-    def fill(p, _):
-        k = code_smem[p, slots + 1]
-        at = count_ref[k]
-        for r in range(slots):
-            list_ref[k * capacity + at + r] = code_smem[p, r]
-        count_ref[k] = at + code_smem[p, slots]
-        return 0
-
-    lax.fori_loop(0, 2 * ndev, fill, 0)
-    for k in range(nlists):
-        at = count_ref[k]
+    start, done = jnp.int32(0), 0
+    for k, size in enumerate(sizes):
+
+        def fill(i, at):
+            p = order_ref[i] ^ me
+            for row in (p, ndev + p):
+                for r in range(slots):
+                    list_ref[at + r] = code_smem[row, r]
+                at = at + code_smem[row, slots]
+            return at
+
+        end = lax.fori_loop(done, done + size, fill, start)
+        done += size
         for r in range(GROUP):
-            list_ref[k * capacity + at + r] = (npairs + ndev * stride) * (1 << 20)
-
-
-def plan(slots, stride, nlists, me, table, mine, came, mask, data):
-    ndev, npairs, nblocks = mine.shape[0], mask.shape[0], data.shape[0] // 6
-    capacity = npairs + ndev * slots + slots + GROUP
-    out = pl.pallas_call(
-        functools.partial(plan_kernel, slots, stride, nlists, capacity),
+            list_ref[end + r] = (npairs + ndev * stride) * (1 << 20)
+        groups = (end - start + GROUP - 1) // GROUP
+        where_ref[2 * k] = start
+        where_ref[2 * k + 1] = groups
+        start = start + groups * GROUP
+
+
+def plan(slots, stride, lists, nblocks, me, mine, came, mask):
+    ndev, npairs = mine.shape[0], mask.shape[0]
+    order = np.array(sum(lists, []), np.int32)
+    table = np.zeros((1, ndev), np.int32)
+    for tags in lists:
+        table[0, tags] = np.arange(len(tags)) * nblocks
+    length = npairs + ndev * slots + len(lists) * GROUP + slots + GROUP
+    return pl.pallas_call(
+        functools.partial(plan_kernel, slots, stride, [len(tags) for tags in lists]),
         out_shape=(
-            jax.ShapeDtypeStruct((nlists * capacity,), I32),
-            jax.ShapeDtypeStruct((nlists,), I32),
+            jax.ShapeDtypeStruct((length,), I32),
+            jax.ShapeDtypeStruct((2 * len(lists),), I32),
             jax.ShapeDtypeStruct((npairs + ndev * stride + 8, 128), F32),
-            jax.ShapeDtypeStruct((nblocks, 64, 256), BF16),
         ),
-        in_specs=[SMEM] + [VMEM] * 5,
-        out_specs=(SMEM, SMEM, VMEM, VMEM),
+        in_specs=[SMEM] * 2 + [VMEM] * 4,
+        out_specs=(SMEM, SMEM, VMEM),
         scratch_shapes=[pltpu.VMEM((2 * ndev, 128), I32), pltpu.SMEM((2 * ndev, 128), I32), pltpu.SemaphoreType.DMA],
         compiler_params=params(16),
         name="plan",
-    )(me, table, mine, came, mask, data)
-    return capacity, out
+    )(me, jnp.asarray(order), jnp.asarray(table), mine, came, mask)
 
 
 def halves(c):
@@ -238,7 +260,7 @@
 def prepare(codes, block_ref, masks_ref, npairs, k_ref, f_ref):
     row = iota((8, 128), 0)
     for g, code in enumerate(codes):
-        d = block_ref[pl.ds((code & 0x3FFF) * 6, 8), :]
+        d = load_block(block_ref, code & 0x3FFF)
         left, sums = other_features(d, row)
         place = code >> 20
         mask = jnp.where(place < npairs, 1.0, masks_ref[pl.ds(place, 1), :])
@@ -274,9 +296,7 @@
     row = iota((8, 128), 0)
 
     def block(b, _):
-        start = jnp.minimum(b * 6, nblocks * 6 - 8)
-        d = data_ref[pl.ds(start, 8), :]
-        d = jnp.where(b == nblocks - 1, pltpu.roll(d, 6, 0), d)
+        d = load_block(data_ref, b)
         acc = acc_ref[b]
 
         def sums(a):
@@ -297,8 +317,8 @@
     lax.fori_loop(0, nblocks, block, 0)
 
 
-def task_kernel(lists, capacity, npairs, first, last, *refs):
-    list_ref, count_ref, masks_ref, own_ref, data_ref = refs[:5]
+def task_kernel(lists, npairs, first, last, *refs):
+    list_ref, where_ref, masks_ref, own_ref, data_ref = refs[:5]
     blocks, refs = refs[5 : 5 + len(lists)], refs[5 + len(lists) :]
     if not first:
         before_ref, refs = refs[0], refs[1:]
@@ -311,11 +331,10 @@
     else:
         acc_ref[...] = before_ref[...]
     for k, block_ref in zip(lists, blocks):
-        count = count_ref[k]
-        groups = (count + GROUP - 1) // GROUP
-
-        def codes(i, k=k):
-            return [list_ref[k * capacity + i * GROUP + g] for g in range(GROUP)]
+        start, groups = where_ref[2 * k], where_ref[2 * k + 1]
+
+        def codes(i, start=start):
+            return [list_ref[start + i * GROUP + g] for g in range(GROUP)]
 
         @pl.when(groups > 0)
         def _(block_ref=block_ref, codes=codes, groups=groups):
@@ -332,7 +351,7 @@
         finish(data_ref, acc_ref, grad_ref, hess_ref)
 
 
-def tasks(lists, capacity, npairs, list_, count, masks, own, data, blocks, before, last):
+def tasks(lists, npairs, list_, where, masks, own, data, blocks, before, last):
     nblocks = own.shape[0]
     acc = jax.ShapeDtypeStruct((nblocks, 16, 256), F32)
     out = jax.ShapeDtypeStruct((3, nblocks, 128), F32)
@@ -340,10 +359,10 @@
     scratch = [pltpu.VMEM((GROUP, 128, 64), BF16), pltpu.VMEM((GROUP, 16, 128), BF16)]
     if last:
         scratch = [pltpu.VMEM(acc.shape, F32)] + scratch
-    args = [list_, count, masks, own, data, *blocks] + ([] if first else [before])
+    args = [list_, where, masks, own, data, *blocks] + ([] if first else [before])
     size = sum(b.size for b in blocks) * 4
     return pl.pallas_call(
-        functools.partial(task_kernel, lists, capacity, npairs, first, last),
+        functools.partial(task_kernel, lists, npairs, first, last),
         out_shape=(out, out) if last else acc,
         in_specs=[SMEM, SMEM] + [VMEM] * (len(args) - 2),
         out_specs=(VMEM, VMEM) if last else VMEM,
@@ -358,10 +377,6 @@
     def __init__(self, tags, array):
         self.tags, self.array = list(tags), array
 
-    def cut(self, start, stop):
-        rows = self.array.shape[0] // len(self.tags)
-        return Piece(self.tags[start:stop], self.array[start * rows : stop * rows])
-
 
 def join(pieces):
     if len(pieces) == 1:
@@ -372,11 +387,6 @@
 def swap(piece, bit, ndev):
     pairs = [(i, i ^ (1 << bit)) for i in range(ndev)]
     return Piece([t ^ (1 << bit) for t in piece.tags], lax.ppermute(piece.array, AXES, pairs))
-
-
-def tie(piece, other):
-    array, _ = lax.optimization_barrier((piece.array, other))
-    return Piece(piece.tags, array)
 
 
 def on_device(positions, direction, pair_local, pair_peer, pair_remote, pair_mask):
@@ -390,6 +400,7 @@
     data = weave(positions, direction)
     send, mine = pack(ndev, slots, stride, peer, local, remote, pair_mask, data)
     came = lax.all_to_all(send, AXES, split_axis=0, concat_axis=0, tiled=True)
+    own = features(data)
 
     bits = ndev.bit_length() - 1
     x, y = bits - 2, bits - 1
@@ -397,48 +408,27 @@
     for bit in range(bits - 3, 0, -1):
         column = join([column, swap(column, bit, ndev)])
     column.array, came = lax.optimization_barrier((column.array, came))
+
+    over_x, over_y = [t ^ (1 << x) for t in column.tags], [t ^ (1 << y) for t in column.tags]
+    corner = [t ^ (1 << x) for t in over_y]
+    lists = []
+    for tags in (column.tags, over_x, over_y, corner):
+        lists += [list(tags), [tag ^ 1 for tag in tags]]
+    list_, where, masks = plan(slots, stride, lists, nblocks, me.reshape(1), mine, came, pair_mask)
+    run = functools.partial(tasks, npairs=npairs, list_=list_, where=where, masks=masks, own=own, data=data)
+
     over_x, over_y = swap(column, x, ndev), swap(column, y, ndev)
-    half = len(column.tags) // 2
-
-    table = np.zeros((1, ndev), np.int32)
-    tail = Piece([], jnp.zeros((8, 128), F32))
-
-    def both(k, pieces):
-        near = join(pieces + [tail])
-        far = swap(near, 0, ndev)
-        for which, p in ((2 * k, near), (2 * k + 1, far)):
-            for unit, tag in enumerate(p.tags):
-                table[0, tag] = which * 256 + unit
-        return near.array, far.array
-
-    shape = [
-        [column],
-        [Piece([t ^ (1 << x) for t in column.tags], None), Piece([t ^ (1 << y) for t in column.tags], None)],
-    ]
-    diagonal = [t ^ (1 << x) ^ (1 << y) for t in column.tags]
-    shape.append([Piece(diagonal[:half], None), Piece(diagonal[half:], None)])
-    for k, pieces in enumerate(shape):
-        tags = sum([p.tags for p in pieces], [])
-        for unit, tag in enumerate(tags):
-            table[0, tag] = 2 * k * 256 + unit
-            table[0, tag ^ 1] = (2 * k + 1) * 256 + unit
-    nlists = 6
-    capacity, (list_, count, masks, own) = plan(
-        slots, stride, nlists, me.reshape(1), jnp.asarray(table), mine, came, pair_mask, data
-    )
-    run = functools.partial(tasks, capacity=capacity, npairs=npairs, list_=list_, count=count, masks=masks, own=own, data=data)
-
-    near, far = both(0, [column])
-    acc = run(lists=(0, 1), blocks=(near, far), before=None, last=False)
-    over_x, over_y = tie(over_x, acc), tie(over_y, acc)
-    corner_x, corner_y = swap(over_y.cut(0, half), x, ndev), swap(over_x.cut(half, 2 * half), y, ndev)
-    near, far = both(1, [over_x, over_y])
-    acc = run(lists=(2,), blocks=(near,), before=acc, last=False)
-    acc = run(lists=(3,), blocks=(far,), before=acc, last=False)
-    corner_x, corner_y = tie(corner_x, acc), tie(corner_y, acc)
-    near, far = both(2, [corner_x, corner_y])
-    acc = run(lists=(4,), blocks=(near,), before=acc, last=False)
-    return run(lists=(5,), blocks=(far,), before=acc, last=True)
+    twin = swap(column, 0, ndev)
+    acc = run(lists=(0, 1), blocks=(column.array, twin.array), before=None, last=False)
+    over_x.array, over_y.array, acc = lax.optimization_barrier((over_x.array, over_y.array, acc))
+    corner = swap(over_y, x, ndev)
+    twin_x, twin_y = swap(over_x, 0, ndev), swap(over_y, 0, ndev)
+    acc = run(lists=(2, 4), blocks=(over_x.array, over_y.array), before=acc, last=False)
+    acc = run(lists=(3, 5), blocks=(twin_x.array, twin_y.array), before=acc, last=False)
+    corner.array, acc = lax.optimization_barrier((corner.array, acc))
+    twin = swap(corner, 0, ndev)
+    acc = run(lists=(6,), blocks=(corner.array,), before=acc, last=False)
+    return run(lists=(7,), blocks=(twin.array,), before=acc, last=True)
 
 
 def solution(mesh):

time: 109 us -> 99.2 us (0.910)
  the two profiles are of different devices: /device:TPU:27 before, /device:TPU:4 now
where the time goes in v1:
time: 99.2 us; the launch traced here: 97.8 us
  Pallas kernels  67 us (68%)
  waiting for transfers between devices  13.9 us (14%)
  starting transfers between devices  13.2 us (13%)
  other arithmetic  1.93 us (2%)
    pallas_call x5, Pallas kernels, tasks(): pl.pallas_call(functools.partial(task_kernel, lists, npairs, first, last)...  58.2 us
    ppermute x9, waiting for transfers between devices, swap(): lax.ppermute(piece.array, AXES, pairs)  13.9 us
    ppermute x9, starting transfers between devices, swap(): lax.ppermute(piece.array, AXES, pairs)  9.13 us
    all_to_all x1, starting transfers between devices, on_device(): came = lax.all_to_all(send, AXES, split_axis=0, concat_axis=0, tiled=True)  4.08 us
    pallas_call x1, Pallas kernels, plan(): pl.pallas_call(functools.partial(plan_kernel, slots, stride, [len(tags) f...  3.89 us
    pallas_call x1, Pallas kernels, pack(): pl.pallas_call(functools.partial(pack_kernel, ndev, slots, stride), out_s...  2.45 us
  transfers between devices with their start and end apart: 10, of which 2 were waited for; matrix products, arithmetic and copies ran while one was open for 2% of the time, Pallas kernels for 58%

profile of v1, /device:TPU:4, one launch (start us, length us, event | category | flops | bytes accessed | tf_op | source)
XLA Modules:
  0.0 97.8 jit_solution(18322184781218558331)
XLA Ops:
  0.6 1.6 %weave.1.data_hbm.data_ref.refs_4_ = f32[384,128]{1,0:T(8,128)} custom-call(f32[3,64,128]{2,1,0:T(8,128)} %pos_hbm.1, f32[3,64,128]{2,1,0:T(8,128)} %dir_hbm.1), custom_call_target="tpu_custom_call" | custom-call | tf_op jit(solution)/shard_map/weave/pallas_call | solution.py:48
  2.3 2.7 %collective-permute-start = (f32[384,128]{1,0:T(8,128)}, f32[384,128]{1,0:T(8,128)S(1)}, u32[]{:S(2)}, u32[]{:S(2)}) collective-permute-start(f32[384,128]{1,0:T(8,128)} %weave.1.data_hbm.data_ref.refs_4_), channel_id=1, source_target_pairs={{0,4},{1,5},{2,6},{3,7},{4,0},{5,1},{6,2},{7,3},{8,12},{9,13},{10,... | collective-permute-start | bytes 589832 | tf_op jit(solution)/shard_map/ppermute | solution.py:389
  4.9 2.4 %pack.1 = (f32[768,128]{1,0:T(8,128)}, f32[32,128]{1,0:T(8,128)}) custom-call(s32[1,256]{1,0:T(1,128)} %bitcast.8, s32[1,256]{1,0:T(1,128)} %bitcast.9, s32[1,256]{1,0:T(1,128)} %bitcast.10, s32[256,128]{1,0:T(8,128)} %mask_ref.1, f32[384,128]{1,0:T(8,128)} %weave.1.data_hbm.data_ref.refs_4_), custom_call_target="tpu_custom_call" | custom-call | tf_op jit(solution)/shard_map/pack/pallas_call | solution.py:93
  7.4 4.1 %all-to-all-start = ((f32[32,24,128]{2,1,0:T(8,128)}), f32[32,24,128]{2,1,0:T(8,128)S(1)}, u32[]{:S(2)}, u32[]{:S(2)}) async-start(f32[32,24,128]{2,1,0:T(8,128)} %bitcast.7), calls=%async_computation | async-start | bytes 786432 | tf_op jit(solution)/shard_map/all_to_all | solution.py:402
  11.5 2.9 %collective-permute-done = f32[384,128]{1,0:T(8,128)S(1)} collective-permute-done((f32[384,128]{1,0:T(8,128)}, f32[384,128]{1,0:T(8,128)S(1)}, u32[]{:S(2)}, u32[]{:S(2)}) %collective-permute-start) | collective-permute-done | bytes 196640 | tf_op jit(solution)/shard_map/ppermute | solution.py:389
  14.3 1.0 pad_maximum_fusion.1
  15.3 0.0 copy-start.2
  15.3 0.0 copy-start.3
  15.3 0.0 copy-start.4
  15.3 3.7 %collective-permute-start.1 = (f32[768,128]{1,0:T(8,128)S(1)}, f32[768,128]{1,0:T(8,128)S(1)}, u32[]{:S(2)}, u32[]{:S(2)}) collective-permute-start(f32[768,128]{1,0:T(8,128)S(1)} %pad_maximum_fusion.1), channel_id=1, source_target_pairs={{0,2},{1,3},{2,0},{3,1},{4,6},{5,7},{6,4},{7,5},{8,10},{9,11},{10,... | collective-permute-start | bytes 1179656 | tf_op jit(solution)/shard_map/ppermute | solution.py:389
  19.0 11.0 %collective-permute-done.1 = f32[768,128]{1,0:T(8,128)S(1)} collective-permute-done((f32[768,128]{1,0:T(8,128)S(1)}, f32[768,128]{1,0:T(8,128)S(1)}, u32[]{:S(2)}, u32[]{:S(2)}) %collective-permute-start.1) | collective-permute-done | bytes 393248 | tf_op jit(solution)/shard_map/ppermute | solution.py:389
  30.1 1.0 %pad_maximum_fusion.refs_5_ = f32[1536,128]{1,0:T(8,128)S(1)} fusion(f32[768,128]{1,0:T(8,128)S(1)} %collective-permute-done.1, f32[384,128]{1,0:T(8,128)S(1)} %collective-permute-done, f32[384,128]{1,0:T(8,128)} %weave.1.data_hbm.data_ref.refs_4_), kind=kLoop, calls=%fused_computation | loop fusion | flops 393216 | bytes 1572864 | tf_op jit(solution)/shard_map/concatenate | solution.py:384
  31.0 0.0 all-to-all-done
  31.0 0.1 collective-permute-start.4
  31.1 0.6 collective-permute-start.3
  31.8 1.4 %collective-permute-start.2 = (f32[1536,128]{1,0:T(8,128)S(1)}, f32[1536,128]{1,0:T(8,128)}, u32[]{:S(2)}, u32[]{:S(2)}) collective-permute-start(f32[1536,128]{1,0:T(8,128)S(1)} %pad_maximum_fusion.refs_5_), channel_id=1, source_target_pairs={{0,8},{1,9},{2,10},{3,11},{4,12},{5,13},{6,14},{7,15},{8,0},{9,1},... | collective-permute-start | bytes 2359304 | tf_op jit(solution)/shard_map/ppermute | solution.py:389
  33.2 0.8 features.1.refs_3_
  34.0 0.0 copy-start.1
  34.0 0.9 copy-done.1
  34.9 3.9 %plan.1 = (s32[928]{0:T(1024)S(1)}, s32[16]{0:T(128)S(1)}, f32[1032,128]{1,0:T(8,128)S(1)}) custom-call(s32[1]{0:T(128)} %bitcast.me_ref, s32[32]{0:T(128)S(1)} %copy-done.4, s32[1,32]{1,0:T(1,128)S(1)} %copy-done.3, f32[32,128]{1,0:T(8,128)S(1)} %copy-done.2, f32[768,128]{1,0:T(8,128)S(1)} %bitcast.6, s32[256,128]{1,0:T(8,128)S(1)} %copy-done.1), custom_call_target="tpu_custom_call" | custom-call | tf_op jit(solution)/shard_map/plan/pallas_call | solution.py:240
  38.8 0.0 collective-permute-done.4.refs_6_
  38.8 15.5 %tasks.5.refs_7_ = f32[64,16,256]{2,1,0:T(8,128)S(1)} custom-call(s32[928]{0:T(1024)S(1)} %get-tuple-element.17.refs_0_, s32[16]{0:T(128)S(1)} %get-tuple-element.18.refs_1_, f32[1032,128]{1,0:T(8,128)S(1)} %get-tuple-element.19.refs_2_, bf16[64,64,256]{2,1,0:T(8,128)(2,1)S(1)} %features.1.refs_3_, f32[384,128]{1,0:T(8,128)S(1)} %copy-done, ...), custom_call_target="tpu_custom_call" | custom-call | flops 3145728000 | bytes 4718592 | tf_op jit(solution)/shard_map/tasks/pallas_call | solution.py:364
  54.3 0.0 collective-permute-done.3.refs_6_
  54.3 0.1 collective-permute-start.6
  54.4 0.5 collective-permute-start.7
  54.9 13.8 %tasks.6.refs_7_ = f32[64,16,256]{2,1,0:T(8,128)S(1)} custom-call(s32[928]{0:T(1024)S(1)} %get-tuple-element.17.refs_0_, s32[16]{0:T(128)S(1)} %get-tuple-element.18.refs_1_, f32[1032,128]{1,0:T(8,128)S(1)} %get-tuple-element.19.refs_2_, bf16[64,64,256]{2,1,0:T(8,128)(2,1)S(1)} %features.1.refs_3_, f32[384,128]{1,0:T(8,128)S(1)} %copy-done, ...), custom_call_target="tpu_custom_call" | custom-call | flops 3145728000 | bytes 4718592 | tf_op jit(solution)/shard_map/tasks/pallas_call | solution.py:364
  68.7 0.0 collective-permute-done.6.refs_5_
  68.7 0.0 collective-permute-done.7.refs_6_
  68.7 14.0 %tasks.7.refs_6_ = f32[64,16,256]{2,1,0:T(8,128)S(1)} custom-call(s32[928]{0:T(1024)S(1)} %get-tuple-element.17.refs_0_, s32[16]{0:T(128)S(1)} %get-tuple-element.18.refs_1_, f32[1032,128]{1,0:T(8,128)S(1)} %get-tuple-element.19.refs_2_, bf16[64,64,256]{2,1,0:T(8,128)(2,1)S(1)} %features.1.refs_3_, f32[384,128]{1,0:T(8,128)S(1)} %copy-done, ...), custom_call_target="tpu_custom_call" | custom-call | flops 3145728000 | bytes 4718592 | tf_op jit(solution)/shard_map/tasks/pallas_call | solution.py:364
  82.7 0.1 collective-permute-start.8
  82.7 6.8 %tasks.8.refs_6_ = f32[64,16,256]{2,1,0:T(8,128)S(1)} custom-call(s32[928]{0:T(1024)S(1)} %get-tuple-element.17.refs_0_, s32[16]{0:T(128)S(1)} %get-tuple-element.18.refs_1_, f32[1032,128]{1,0:T(8,128)S(1)} %get-tuple-element.19.refs_2_, bf16[64,64,256]{2,1,0:T(8,128)(2,1)S(1)} %features.1.refs_3_, f32[384,128]{1,0:T(8,128)S(1)} %copy-done, ...), custom_call_target="tpu_custom_call" | custom-call | flops 1572864000 | bytes 2359296 | tf_op jit(solution)/shard_map/tasks/pallas_call | solution.py:364
  89.6 8.2 %tasks.9 = (f32[3,64,128]{2,1,0:T(8,128)}, f32[3,64,128]{2,1,0:T(8,128)}) custom-call(s32[928]{0:T(1024)S(1)} %get-tuple-element.17.refs_0_, s32[16]{0:T(128)S(1)} %get-tuple-element.18.refs_1_, f32[1032,128]{1,0:T(8,128)S(1)} %get-tuple-element.19.refs_2_, bf16[64,64,256]{2,1,0:T(8,128)(2,1)S(1)} %features.1.refs_3_, f32[384,128]{1,0:T(8,128)S(1)} %copy-done, ...), custom_call_target="tpu_custom_call" | custom-call | flops 1572864000 | bytes 2359296 | tf_op jit(solution)/shard_map/tasks/pallas_call | solution.py:364
  (9 shorter events, 0.0 us)
Async XLA Ops:
  2.3 30.9 %copy-start = (f32[384,128]{1,0:T(8,128)S(1)}, f32[384,128]{1,0:T(8,128)}, u32[]{:S(2)}) copy-start(f32[384,128]{1,0:T(8,128)} %weave.1.data_hbm.data_ref.refs_4_) | copy-start | bytes 589828
  2.3 12.1 %collective-permute-start = (f32[384,128]{1,0:T(8,128)}, f32[384,128]{1,0:T(8,128)S(1)}, u32[]{:S(2)}, u32[]{:S(2)}) collective-permute-start(f32[384,128]{1,0:T(8,128)} %weave.1.data_hbm.data_ref.refs_4_), channel_id=1, source_target_pairs={{0,4},{1,5},{2,6},{3,7},{4,0},{5,1},{6,2},{7,3},{8,12},{9,13},{10,... | collective-permute-start | bytes 589832 | tf_op jit(solution)/shard_map/ppermute | solution.py:389
  7.4 23.6 %all-to-all-start = ((f32[32,24,128]{2,1,0:T(8,128)}), f32[32,24,128]{2,1,0:T(8,128)S(1)}, u32[]{:S(2)}, u32[]{:S(2)}) async-start(f32[32,24,128]{2,1,0:T(8,128)} %bitcast.7), calls=%async_computation | async-start | bytes 786432 | tf_op jit(solution)/shard_map/all_to_all | solution.py:402
  15.3 18.7 %copy-start.2 = (f32[32,128]{1,0:T(8,128)S(1)}, f32[32,128]{1,0:T(8,128)}, u32[]{:S(2)}) copy-start(f32[32,128]{1,0:T(8,128)} %get-tuple-element.14.mine_ref) | copy-start | bytes 49156
  15.3 18.7 %copy-start.3 = (s32[1,32]{1,0:T(1,128)S(1)}, s32[1,32]{1,0:T(1,128)}, u32[]{:S(2)}) copy-start(s32[1,32]{1,0:T(1,128)} %constant.15.clone.table_ref) | copy-start | bytes 388
  15.3 18.7 %copy-start.4 = (s32[32]{0:T(128)S(1)}, s32[32]{0:T(128)}, u32[]{:S(2)}) copy-start(s32[32]{0:T(128)} %constant.14.clone.order_ref) | copy-start | bytes 388
  15.3 14.7 %collective-permute-start.1 = (f32[768,128]{1,0:T(8,128)S(1)}, f32[768,128]{1,0:T(8,128)S(1)}, u32[]{:S(2)}, u32[]{:S(2)}) collective-permute-start(f32[768,128]{1,0:T(8,128)S(1)} %pad_maximum_fusion.1), channel_id=1, source_target_pairs={{0,2},{1,3},{2,0},{3,1},{4,6},{5,7},{6,4},{7,5},{8,10},{9,11},{10,... | collective-permute-start | bytes 1179656 | tf_op jit(solution)/shard_map/ppermute | solution.py:389
  31.0 7.8 %collective-permute-start.4 = (f32[1536,128]{1,0:T(8,128)S(1)}, f32[1536,128]{1,0:T(8,128)}, u32[]{:S(2)}, u32[]{:S(2)}) collective-permute-start(f32[1536,128]{1,0:T(8,128)S(1)} %pad_maximum_fusion.refs_5_), channel_id=1, source_target_pairs={{0,1},{1,0},{2,3},{3,2},{4,5},{5,4},{6,7},{7,6},{8,9},{9,8},{10,11... | collective-permute-start | bytes 2359304 | tf_op jit(solution)/shard_map/ppermute | solution.py:389
  31.1 23.2 %collective-permute-start.3 = (f32[1536,128]{1,0:T(8,128)S(1)}, f32[1536,128]{1,0:T(8,128)}, u32[]{:S(2)}, u32[]{:S(2)}) collective-permute-start(f32[1536,128]{1,0:T(8,128)S(1)} %pad_maximum_fusion.refs_5_), channel_id=1, source_target_pairs={{0,16},{1,17},{2,18},{3,19},{4,20},{5,21},{6,22},{7,23},{8,24},{9,... | collective-permute-start | bytes 2359304 | tf_op jit(solution)/shard_map/ppermute | solution.py:389
  31.8 22.6 %collective-permute-start.2 = (f32[1536,128]{1,0:T(8,128)S(1)}, f32[1536,128]{1,0:T(8,128)}, u32[]{:S(2)}, u32[]{:S(2)}) collective-permute-start(f32[1536,128]{1,0:T(8,128)S(1)} %pad_maximum_fusion.refs_5_), channel_id=1, source_target_pairs={{0,8},{1,9},{2,10},{3,11},{4,12},{5,13},{6,14},{7,15},{8,0},{9,1},... | collective-permute-start | bytes 2359304 | tf_op jit(solution)/shard_map/ppermute | solution.py:389
  34.0 0.9 copy-start.1
  54.3 14.3 %collective-permute-start.6 = (f32[1536,128]{1,0:T(8,128)}, f32[1536,128]{1,0:T(8,128)S(1)}, u32[]{:S(2)}, u32[]{:S(2)}) collective-permute-start(f32[1536,128]{1,0:T(8,128)} %collective-permute-done.2.refs_5_), channel_id=1, source_target_pairs={{0,1},{1,0},{2,3},{3,2},{4,5},{5,4},{6,7},{7,6},{8,9},{9,8},{10,11... | collective-permute-start | bytes 2359304 | tf_op jit(solution)/shard_map/ppermute | solution.py:389
  54.4 14.3 %collective-permute-start.7 = (f32[1536,128]{1,0:T(8,128)}, f32[1536,128]{1,0:T(8,128)S(1)}, u32[]{:S(2)}, u32[]{:S(2)}) collective-permute-start(f32[1536,128]{1,0:T(8,128)} %collective-permute-done.3.refs_6_), channel_id=1, source_target_pairs={{0,1},{1,0},{2,3},{3,2},{4,5},{5,4},{6,7},{7,6},{8,9},{9,8},{10,11... | collective-permute-start | bytes 2359304 | tf_op jit(solution)/shard_map/ppermute | solution.py:389
  54.9 27.8 %collective-permute-start.5 = (f32[1536,128]{1,0:T(8,128)}, f32[1536,128]{1,0:T(8,128)S(1)}, u32[]{:S(2)}, u32[]{:S(2)}) collective-permute-start(f32[1536,128]{1,0:T(8,128)} %collective-permute-done.3.refs_6_), channel_id=1, source_target_pairs={{0,8},{1,9},{2,10},{3,11},{4,12},{5,13},{6,14},{7,15},{8,0},{9,1},... | collective-permute-start | bytes 2359304 | tf_op jit(solution)/shard_map/ppermute | solution.py:389
  82.7 6.9 %collective-permute-start.8 = (f32[1536,128]{1,0:T(8,128)S(1)}, f32[1536,128]{1,0:T(8,128)S(1)}, u32[]{:S(2)}, u32[]{:S(2)}) collective-permute-start(f32[1536,128]{1,0:T(8,128)S(1)} %collective-permute-done.5.refs_5_), channel_id=1, source_target_pairs={{0,1},{1,0},{2,3},{3,2},{4,5},{5,4},{6,7},{7,6},{8,9},{9,8},{10,11... | collective-permute-start | bytes 2359304 | tf_op jit(solution)/shard_map/ppermute | solution.py:389
